TPU v7x, 32 devices: a whole 2x2x4 slice. The times are simulated.
32 devices in a mesh: groups: 2 (over y), seq: 4 (over z), dp: 2 (over x), head: 2 (over core).
Axes of the slice: x: 2, y: 2, z: 4, core: 2. Of those that a mesh axis runs over, the one named last changes fastest.
Arguments:
- latents: bfloat16 [4, 8, 512, 1024], P(('groups', 'dp'), None, 'seq', 'head'), parts along dimension 0, may hold values from -6 to 6
- log_decay: bfloat16 [4, 8, 512, 8], P(('groups', 'dp'), None, 'seq', 'head'), parts along dimension 0, may hold values from -1 to 0, as said below
- seg_lengths: int32 [4, 4], P(('groups', 'dp')), parts along dimension 0, may hold values from 1 to 2048, 4096 in all within a row
- qkv_weight: bfloat16 [1024, 3, 1024], P('seq', None, 'head'), may hold values from -0.1875 to 0.1875
- out_weight: bfloat16 [1024, 1024], P('seq', 'head'), may hold values from -0.1875 to 0.1875
- cotangent: bfloat16 [4, 8, 512, 1024], P(('groups', 'dp'), 'seq', None, 'head'), parts along dimension 0, may hold values from -6 to 6
Outputs:
- layer_out: bfloat16 [4, 8, 512, 1024], P(('groups', 'dp'), 'seq', None, 'head'), parts along dimension 0
- output_weight_gradient: float32 [2048, 1024], P(('groups', 'seq'), 'head'), parts along dimension 0
There are 2 independent parts, one for each index of `groups`. A program takes and returns all parts, laid end to end along the dimension named above; an argument that names none is the same for every part. Nothing has to cross between parts.
Inputs may be any that keep to these rules, and one draw needn't show every extreme that they name: `log_decay`: never positive. `seg_lengths`: each row sums to 4096; a segment's state is reset at its first token.
All inputs are finite; a program needn't handle non-finite values.
Results may differ from a plain program's by a relative error of at most 0.0073.
Values may be sent and summed in bfloat16 or wider, within the bound.
A program may use at most 64 MiB of HBM per device.

v0:
```python
from functools import partial
import jax
import jax.numpy as jnp
from jax import lax
from jax.sharding import PartitionSpec as P


def shifted(value, axis, steps):
    count = lax.axis_size(axis)
    initial, last = (max(0, -steps), min(count, count - steps))
    return lax.ppermute(value, axis, [(source, source + steps) for source in range(initial, last)])


def block_step(carry_state, queries, key_rows, values_in, log_rates, segment, previous):
    head_scale = queries.shape[-1] ** (-0.5)
    cumulative = jnp.cumsum(log_rates, axis=-1)
    size_here = log_rates.shape[-1]
    order_idx = jnp.arange(size_here)
    allowed = (order_idx[:, None] >= order_idx[None, :]) & (segment[:, None] == segment[None, :])
    spread = cumulative[:, :, None] - cumulative[:, None, :]
    weight = jnp.where(allowed[None], jnp.exp(jnp.where(allowed[None], spread, 0.0)), 0.0)
    scores = jnp.einsum("htd,hsd->hts", queries, key_rows, preferred_element_type=jnp.float32)
    mixing = (scores * head_scale * weight).astype(jnp.bfloat16)
    inner_sum = jnp.einsum("hts,hsd->htd", mixing, values_in, preferred_element_type=jnp.float32)
    kept_mask = (segment == previous).astype(jnp.float32)
    carried = jnp.einsum(
        "htd,hde->hte", queries.astype(jnp.float32), carry_state, precision=lax.Precision.HIGHEST
    )
    result = (
        inner_sum
        + kept_mask[None, :, None] * jnp.exp(cumulative)[:, :, None] * carried * head_scale
    )
    last_seg = segment[-1]
    tail_decay = (
        jnp.exp(cumulative[:, -1:] - cumulative)
        * (segment == last_seg).astype(jnp.float32)[None, :]
    )
    decayed = (key_rows.astype(jnp.float32) * tail_decay[:, :, None]).astype(jnp.bfloat16)
    fresh = jnp.einsum("hsd,hse->hde", decayed, values_in, preferred_element_type=jnp.float32)
    through = jnp.exp(cumulative[:, -1]) * (last_seg == previous).astype(jnp.float32)
    return (through[:, None, None] * carry_state + fresh, result)


def to_blocks(array, count):
    moved = array.reshape((array.shape[0], count, array.shape[1] // count) + array.shape[2:])
    return jnp.moveaxis(moved, 1, 0)


def local_pass(queries, key_rows, values_in, log_rates, segment, before, block_size):
    heads_here, length, head_dim = queries.shape
    count = length // block_size
    seg_blocks = segment.reshape(count, block_size)
    previous = jnp.concatenate([jnp.reshape(before, (1,)), seg_blocks[:-1, -1]])

    def advance(carry_state, slab_in):
        q_blk, k_blk, v_blk, r_blk, s_blk, p_blk = slab_in
        return block_step(carry_state, q_blk, k_blk, v_blk, r_blk, s_blk, p_blk)

    start_state = jnp.zeros((heads_here, head_dim, head_dim), jnp.float32)
    final_state, block_outs = lax.scan(
        advance,
        start_state,
        (
            to_blocks(queries, count),
            to_blocks(key_rows, count),
            to_blocks(values_in, count),
            to_blocks(log_rates, count),
            seg_blocks,
            previous,
        ),
    )
    outputs = jnp.moveaxis(block_outs, 0, 1).reshape(heads_here, length, head_dim)
    return (outputs, final_state)


def local(latents, log_decay, seg_lengths, qkv_weight, out_weight, cotangent):
    strips, rate_strips = (
        lax.all_to_all(latents, "seq", split_axis=1, concat_axis=2, tiled=True),
        lax.all_to_all(log_decay, "seq", split_axis=1, concat_axis=2, tiled=True),
    )
    features = lax.all_gather(strips, "head", axis=3, tiled=True)
    proj_full, out_full = (
        lax.all_gather(qkv_weight, "seq", axis=0, tiled=True),
        lax.all_gather(out_weight, "seq", axis=0, tiled=True),
    )
    drives_here, rows_here, columns, feature_width = features.shape
    tokens_here = rows_here * columns
    heads_here = rate_strips.shape[3]
    head_dim = proj_full.shape[2] // heads_here
    block_size = min(512, tokens_here)
    split_weight = proj_full.reshape(feature_width, 3, heads_here, head_dim)
    projected = jnp.einsum(
        "bsaf,fchd->cbhsad", features, split_weight, preferred_element_type=jnp.float32
    ).astype(jnp.bfloat16)
    projected = projected.reshape(3, drives_here, heads_here, tokens_here, head_dim)
    log_rates = jnp.transpose(rate_strips.astype(jnp.float32), (0, 3, 1, 2)).reshape(
        drives_here, heads_here, tokens_here
    )
    starts = jnp.cumsum(seg_lengths, axis=1) - seg_lengths
    first_pos = lax.axis_index("seq") * tokens_here
    position = first_pos + jnp.arange(tokens_here, dtype=jnp.int32)
    segment = jnp.sum((starts[:, :, None] <= position[None, None, :]).astype(jnp.int32), axis=1) - 1
    before = jnp.sum((starts <= first_pos - 1).astype(jnp.int32), axis=1) - 1
    run_local = jax.vmap(partial(local_pass, block_size=block_size))
    local_out, own_state = run_local(
        projected[0], projected[1], projected[2], log_rates, segment, before
    )
    running = jnp.cumsum(log_rates, axis=2)
    joined_seg = (segment[:, -1] == before).astype(jnp.float32)
    self_decay = jnp.exp(running[:, :, -1]) * joined_seg[:, None]

    def relay(step_index, incoming):
        return shifted(self_decay[:, :, None, None] * incoming + own_state, "seq", 1)

    prefix = lax.fori_loop(0, lax.axis_size("seq") - 1, relay, jnp.zeros_like(own_state))
    head_scale = head_dim ** (-0.5)
    kept_mask = (segment == before[:, None]).astype(jnp.float32)
    carried = jnp.einsum(
        "bhtd,bhde->bhte", projected[0].astype(jnp.float32), prefix, precision=lax.Precision.HIGHEST
    )
    combined = (
        local_out
        + kept_mask[:, None, :, None] * jnp.exp(running)[:, :, :, None] * head_scale * carried
    )
    normed = combined * lax.rsqrt(jnp.mean(combined * combined, axis=-1, keepdims=True) + 1e-06)
    attn_rows = jnp.transpose(normed.astype(jnp.bfloat16), (0, 2, 1, 3)).reshape(
        drives_here * tokens_here, heads_here * head_dim
    )
    attn_full = lax.all_gather(attn_rows, "head", axis=1, tiled=True)
    layer_out = jnp.dot(attn_full, out_full, preferred_element_type=jnp.float32).astype(
        jnp.bfloat16
    )
    layer_out = layer_out.reshape(drives_here, rows_here, columns, out_full.shape[1])
    cot_rows = cotangent.reshape(drives_here * tokens_here, cotangent.shape[3])
    factor = float(lax.axis_size("dp") * lax.axis_size("seq") * drives_here * tokens_here) ** (-0.5)
    my_rows = lax.psum_scatter(
        lax.dot_general(
            attn_full, cot_rows, (((0,), (0,)), ((), ())), preferred_element_type=jnp.float32
        )
        * factor,
        "seq",
        scatter_dimension=0,
        tiled=True,
    )
    weight_grad = lax.psum(my_rows, "dp")
    return (layer_out, weight_grad)


def solution(mesh):
    in_specs = (
        P(("groups", "dp"), None, "seq", "head"),
        P(("groups", "dp"), None, "seq", "head"),
        P(("groups", "dp"), None),
        P("seq", None, "head"),
        P("seq", "head"),
        P(("groups", "dp"), "seq", None, "head"),
    )
    out_specs = (P(("groups", "dp"), "seq", None, "head"), P(("groups", "seq"), "head"))
    return jax.shard_map(local, mesh=mesh, in_specs=in_specs, out_specs=out_specs, check_vma=False)
```

profile of v0, /device:TPU:0, one launch (start us, length us, event | category | flops | bytes accessed | tf_op | source)
XLA Modules:
  0.0 310.2 jit_solution(2354458996665151048)
XLA Ops:
  7.2 0.7 all-gather.5.cloned.1.call-update
  8.0 56.2 %all_to_all.27 = bf16[1,8,128,512]{3,2,0,1:T(8,128)(2,1)S(1)} all-to-all(bf16[1,8,128,512]{3,2,0,1:T(8,128)(2,1)} %bitcast.208), channel_id=1, replica_groups=mesh['groups'=2,'seq'=4,'dp'=2,'head'=2] {'seq'}, dimensions={1} | all-to-all | bytes 2097152 | tf_op jit(solution)/shard_map/all_to_all | solution.py:78
  64.1 1.1 copy.67
  65.2 5.1 %all-to-all-start = ((bf16[1,8,128,4]{2,3,0,1:T(4,128)(2,1)}), bf16[1,8,128,4]{2,3,0,1:T(4,128)(2,1)S(1)}, u32[]{:S(2)}, u32[]{:S(2)}) async-start(bf16[1,8,128,4]{2,3,0,1:T(4,128)(2,1)} %bitcast.1), calls=%async_computation | async-start | bytes 16384 | tf_op jit(solution)/shard_map/all_to_all | solution.py:79
  70.4 0.2 reduce_window_sum.81
  70.5 0.6 fusion.38
  71.3 0.7 slice.57
  72.6 0.8 add_bitcast_fusion
  73.4 0.6 slice.64
  74.6 1.4 all-to-all-done
  76.0 1.1 reduce-window.16
  77.2 0.2 copy.84
  77.6 0.2 reduce-window.17
  77.9 0.2 copy.83
  78.1 13.0 %all-gather.5.cloned.1.call-done = bf16[1024,3,512]{2,0,1:T(8,128)(2,1)} async-done(((bf16[256,3,512]{2,0,1:T(8,128)(2,1)}), bf16[1024,3,512]{2,0,1:T(8,128)(2,1)}) %all-gather.5.cloned.1.call-update) | async-done | bytes 3145744 | tf_op jit(solution)/shard_map/all_gather | solution.py:83
  91.1 4.7 %copy.65 = bf16[1024,3,512]{0,2,1:T(8,128)(2,1)} copy(bf16[1024,3,512]{2,0,1:T(8,128)(2,1)} %all-gather.5.cloned.1.call-done) | data formatting | bytes 6291456 | tf_op jit(solution)/shard_map/all_gather | solution.py:83
  95.8 7.3 %all-gather.7.cloned.1.call-done = bf16[1,2,512,1024]{3,2,1,0:T(8,128)(2,1)} async-done(((bf16[1,2,512,512]{3,2,1,0:T(8,128)(2,1)}), bf16[1,2,512,1024]{3,2,1,0:T(8,128)(2,1)}) %all-gather.7.cloned.1.call-update) | async-done | bytes 2097168 | tf_op jit(solution)/shard_map/all_gather | solution.py:81
  103.1 6.1 %convert_bitcast_fusion = bf16[3,1,4,2,512,128]{4,5,3,2,0,1:T(8,128)(2,1)S(1)} fusion(bf16[1024,3,4,128,1]{0,3,4,2,1:T(8,128)(2,1)} %bitcast.204, bf16[1,2,512,1024]{3,2,1,0:T(8,128)(2,1)} %all-gather.7.cloned.1.call-done), kind=kOutput, calls=%fused_computation.48 | convolution fusion | flops 3222798336 | bytes 8388608 | tf_op jit(solution)/shard_map/bsaf,fchd->cbhsad/dot_general | solution.py:92
  109.2 2.2 fusion.41
  111.4 29.2 %while.24 = (s32[]{:T(128)}, f32[1,4,128,128]{3,2,1,0:T(8,128)S(1)}, f32[2,1,4,512,128]{4,3,2,1,0:T(8,128)}, f32[2,1,4,512]{3,2,1,0:T(4,128)S(1)}, s32[2,1,512]{...) while((s32[]{:T(128)}, ...), condition=%wide.region_6.7_spmd.clone, body=%wide.region_3.6_spmd.clone.sunk | while | flops 1015816256 | bytes 14092170 | solution.py:60
  111.4 0.6 constant_dynamic-slice_fusion.12
  111.9 0.6 compare_convert_fusion.6
  112.5 1.2 reduce-window.26
  113.9 0.2 reduce-window.27
  114.4 0.2 fusion.68
  114.6 3.5 %fusion.69 = f32[4,512,128]{2,1,0:T(8,128)S(1)} fusion(f32[4,512]{1,0:T(4,128)S(1)} %get-tuple-element.263, pred[512,512]{1,0:T(8,128)(4,1)S(1)} %fusion.68, bf16[2,1,4,512,128]{3,4,0,2,1:T(8,128)(2,1)} %get-tuple-element.299, s32[]{:T(128)} %get-tuple-element.279, bf16[2,1,4,512,128]{3,4,0,2,1:T(8,128)(2,1)} %get-tuple-element.298, ...), kind=kOutput, calls=%fused_computation.2.clone.1 | convolution fusion | flops 543162368 | bytes 2901504 | tf_op jit(solution)/shard_map/vmap()/while/body/eval_jaxpr/hts,hsd->htd/dot_general | solution.py:24
  118.1 2.8 fusion.70
  121.0 0.6 slice.92
  122.9 0.6 compare_convert_fusion.7
  123.6 1.1 constant_dynamic-slice_fusion.10
  124.7 0.3 copy.100
  125.0 0.9 fusion.67
  126.0 0.6 constant_dynamic-slice_fusion.12
  126.5 0.6 compare_convert_fusion.6
  127.2 1.2 reduce-window.26
  128.5 0.2 reduce-window.27
  129.0 0.2 fusion.68
  129.2 3.5 %fusion.69 = f32[4,512,128]{2,1,0:T(8,128)S(1)} fusion(f32[4,512]{1,0:T(4,128)S(1)} %get-tuple-element.263, pred[512,512]{1,0:T(8,128)(4,1)S(1)} %fusion.68, bf16[2,1,4,512,128]{3,4,0,2,1:T(8,128)(2,1)} %get-tuple-element.299, s32[]{:T(128)} %get-tuple-element.279, bf16[2,1,4,512,128]{3,4,0,2,1:T(8,128)(2,1)} %get-tuple-element.298, ...), kind=kOutput, calls=%fused_computation.2.clone.1 | convolution fusion | flops 543162368 | bytes 2901504 | tf_op jit(solution)/shard_map/vmap()/while/body/eval_jaxpr/hts,hsd->htd/dot_general | solution.py:24
  132.7 2.8 fusion.70
  135.5 0.6 slice.92
  137.5 0.6 compare_convert_fusion.7
  138.2 1.1 constant_dynamic-slice_fusion.10
  139.3 0.3 copy.100
  139.6 0.9 fusion.67
  140.5 2.9 copy.72
  143.4 2.9 reshape.615
  146.3 1.6 copy.76
  147.9 28.2 %while.23 = (s32[]{:T(128)}, f32[1,4,128,128]{3,2,1,0:T(8,128)S(1)}, f32[1,4]{1,0:T(1,128)S(1)}, f32[1,4,128,128]{3,2,1,0:T(8,128)S(1)}, s32[]{:T(128)}) while((s32[]{:T(128)}, f32[1,4,128,128]{3,2,1,0:T(8,128)S(1)}, f32[1,4]{1,0:T(1,128)S(1)}, f32[1,4,128,128]{3,2,1,0:T(8,128)S(1)}, s32[]{:T(128)}) %tuple.57), condition=%wide.region_10.11_spmd, body=%wide.region_9.10_spmd.sunk | while | flops 131074 | bytes 1835125 | solution.py:115
  148.0 3.7 %collective-permute-start = (f32[1,4,128,128]{3,2,1,0:T(8,128)S(1)}, f32[1,4,128,128]{3,2,1,0:T(8,128)S(1)}, u32[]{:S(2)}, u32[]{:S(2)}) collective-permute-start(f32[1,4,128,128]{3,2,1,0:T(8,128)S(1)} %multiply_add_fusion.3), channel_id=1, source_target_pairs={{0,4},{4,8},{8,12},{1,5},{5,9},{9,13},{2,6},{6,10},{10,14},{3,7},{... | collective-permute-start | bytes 786440 | tf_op jit(solution)/shard_map/while/body/eval_jaxpr/ppermute | solution.py:11
  151.7 6.0 %collective-permute-done = f32[1,4,128,128]{3,2,1,0:T(8,128)S(1)} collective-permute-done((f32[1,4,128,128]{3,2,1,0:T(8,128)S(1)}, f32[1,4,128,128]{3,2,1,0:T(8,128)S(1)}, u32[]{:S(2)}, u32[]{:S(2)}) %collective-permute-start) | collective-permute-done | bytes 262176 | tf_op jit(solution)/shard_map/while/body/eval_jaxpr/ppermute | solution.py:11
  157.8 4.4 %collective-permute-start = (f32[1,4,128,128]{3,2,1,0:T(8,128)S(1)}, f32[1,4,128,128]{3,2,1,0:T(8,128)S(1)}, u32[]{:S(2)}, u32[]{:S(2)}) collective-permute-start(f32[1,4,128,128]{3,2,1,0:T(8,128)S(1)} %multiply_add_fusion.3), channel_id=1, source_target_pairs={{0,4},{4,8},{8,12},{1,5},{5,9},{9,13},{2,6},{6,10},{10,14},{3,7},{... | collective-permute-start | bytes 786440 | tf_op jit(solution)/shard_map/while/body/eval_jaxpr/ppermute | solution.py:11
  162.2 5.2 %collective-permute-done = f32[1,4,128,128]{3,2,1,0:T(8,128)S(1)} collective-permute-done((f32[1,4,128,128]{3,2,1,0:T(8,128)S(1)}, f32[1,4,128,128]{3,2,1,0:T(8,128)S(1)}, u32[]{:S(2)}, u32[]{:S(2)}) %collective-permute-start) | collective-permute-done | bytes 262176 | tf_op jit(solution)/shard_map/while/body/eval_jaxpr/ppermute | solution.py:11
  167.5 4.4 %collective-permute-start = (f32[1,4,128,128]{3,2,1,0:T(8,128)S(1)}, f32[1,4,128,128]{3,2,1,0:T(8,128)S(1)}, u32[]{:S(2)}, u32[]{:S(2)}) collective-permute-start(f32[1,4,128,128]{3,2,1,0:T(8,128)S(1)} %multiply_add_fusion.3), channel_id=1, source_target_pairs={{0,4},{4,8},{8,12},{1,5},{5,9},{9,13},{2,6},{6,10},{10,14},{3,7},{... | collective-permute-start | bytes 786440 | tf_op jit(solution)/shard_map/while/body/eval_jaxpr/ppermute | solution.py:11
  171.9 4.3 %collective-permute-done = f32[1,4,128,128]{3,2,1,0:T(8,128)S(1)} collective-permute-done((f32[1,4,128,128]{3,2,1,0:T(8,128)S(1)}, f32[1,4,128,128]{3,2,1,0:T(8,128)S(1)}, u32[]{:S(2)}, u32[]{:S(2)}) %collective-permute-start) | collective-permute-done | bytes 262176 | tf_op jit(solution)/shard_map/while/body/eval_jaxpr/ppermute | solution.py:11
  176.2 2.9 multiply_reduce_fusion
  179.1 1.2 multiply_convert_fusion.3
  180.4 12.6 %all-gather.9.cloned.1.call-done = bf16[1024,1024]{0,1:T(8,128)(2,1)} async-done(((bf16[1024,512]{0,1:T(8,128)(2,1)}), bf16[1024,1024]{0,1:T(8,128)(2,1)}) %all-gather.9.cloned.1.call-update) | async-done | bytes 2097168 | tf_op jit(solution)/shard_map/all_gather | solution.py:129
  193.0 4.1 %convolution_multiply_fusion.1 = f32[1024,512]{1,0:T(8,128)} fusion(bf16[1024,1024]{0,1:T(8,128)(2,1)} %all-gather.9.cloned.1.call-done, bf16[1024,512]{1,0:T(8,128)(2,1)S(1)} %bitcast.196), kind=kOutput, calls=%fused_computation.53 | convolution fusion | flops 1074266112 | bytes 5242880 | tf_op jit(solution)/shard_map/dot_general | solution.py:137
  197.2 0.5 all-gather.11.cloned.1.call-update
  197.8 44.5 %reduce-scatter.2.cloned.1.call-done = f32[256,512]{1,0:T(8,128)} async-done(((f32[1024,512]{1,0:T(8,128)}), f32[256,512]{1,0:T(8,128)}) %reduce-scatter.2.cloned.1.call-update) | async-done | bytes 524304 | tf_op jit(solution)/shard_map/reduce_scatter | solution.py:136
  242.4 28.8 %all-gather.11.cloned.1.call-done = bf16[1024,512]{1,0:T(8,128)(2,1)} async-done(((bf16[256,512]{1,0:T(8,128)(2,1)}), bf16[1024,512]{1,0:T(8,128)(2,1)}) %all-gather.11.cloned.1.call-update) | async-done | bytes 1048592 | tf_op jit(solution)/shard_map/all_gather | solution.py:84
  271.1 3.5 %convolution_convert_fusion = bf16[1024,512]{1,0:T(8,128)(2,1)} fusion(bf16[1024,1024]{0,1:T(8,128)(2,1)S(1)} %copy-done.3, bf16[1024,512]{1,0:T(8,128)(2,1)} %all-gather.11.cloned.1.call-done), kind=kOutput, calls=%fused_computation.54 | convolution fusion | flops 1074266112 | bytes 4194304 | tf_op jit(solution)/shard_map/dot_general | solution.py:130
  274.6 26.9 %all-reduce.2.cloned.1.call-done = f32[256,512]{1,0:T(8,128)} async-done(((f32[256,512]{1,0:T(8,128)}), f32[256,512]{1,0:T(8,128)}) %all-reduce.2.cloned.1.call-update) | async-done | bytes 524304 | tf_op jit(solution)/shard_map/psum | solution.py:145
  301.5 1.9 copy.123
  (69 shorter events, 2.4 us)
Async XLA Ops:
  7.2 185.8 %copy-start = (bf16[1,2,512,512]{3,2,1,0:T(8,128)(2,1)S(1)}, bf16[1,2,512,512]{3,2,1,0:T(8,128)(2,1)}, u32[]{:S(2)}) copy-start(bf16[1,2,512,512]{3,2,1,0:T(8,128)(2,1)} %param.15) | copy-start | bytes 3145732
  7.2 83.9 %all-gather.5.cloned.1.call-start = ((), (), s32[]{:S(2)}) async-start(), calls=%async_computation.3 | async-start | bytes 3932160 | tf_op jit(solution)/shard_map/all_gather | solution.py:83
  7.9 95.2 %all-gather.7.cloned.1.call-start = ((), (), s32[]{:S(2)}) async-start(), calls=%async_computation.4 | async-start | bytes 3145728 | tf_op jit(solution)/shard_map/all_gather | solution.py:81
  64.1 6.2 %copy-start.2 = (s32[1,4]{1,0:T(1,128)S(1)}, s32[1,4]{1,0:T(1,128)}, u32[]{:S(2)}) copy-start(s32[1,4]{1,0:T(1,128)} %param.12) | copy-start | bytes 52
  65.2 10.7 %all-to-all-start = ((bf16[1,8,128,4]{2,3,0,1:T(4,128)(2,1)}), bf16[1,8,128,4]{2,3,0,1:T(4,128)(2,1)S(1)}, u32[]{:S(2)}, u32[]{:S(2)}) async-start(bf16[1,8,128,4]{2,3,0,1:T(4,128)(2,1)} %bitcast.1), calls=%async_computation | async-start | bytes 16384 | tf_op jit(solution)/shard_map/all_to_all | solution.py:79
  70.4 122.6 %all-gather.9.cloned.1.call-start = ((), (), s32[]{:S(2)}) async-start(), calls=%async_computation.5 | async-start | bytes 3145728 | tf_op jit(solution)/shard_map/all_gather | solution.py:129
  120.9 4.1 %copy-start.1 = (bf16[2,1,4,512,128]{3,4,0,2,1:T(8,128)(2,1)S(1)}, bf16[2,1,4,512,128]{3,4,0,2,1:T(8,128)(2,1)}, u32[]{:S(2)}) copy-start(bf16[2,1,4,512,128]{3,4,0,2,1:T(8,128)(2,1)} %get-tuple-element.298) | copy-start | bytes 3145732 | tf_op jit(solution)/shard_map/vmap()/while
  135.5 4.1 %copy-start.1 = (bf16[2,1,4,512,128]{3,4,0,2,1:T(8,128)(2,1)S(1)}, bf16[2,1,4,512,128]{3,4,0,2,1:T(8,128)(2,1)}, u32[]{:S(2)}) copy-start(bf16[2,1,4,512,128]{3,4,0,2,1:T(8,128)(2,1)} %get-tuple-element.298) | copy-start | bytes 3145732 | tf_op jit(solution)/shard_map/vmap()/while
  148.0 9.7 %collective-permute-start = (f32[1,4,128,128]{3,2,1,0:T(8,128)S(1)}, f32[1,4,128,128]{3,2,1,0:T(8,128)S(1)}, u32[]{:S(2)}, u32[]{:S(2)}) collective-permute-start(f32[1,4,128,128]{3,2,1,0:T(8,128)S(1)} %multiply_add_fusion.3), channel_id=1, source_target_pairs={{0,4},{4,8},{8,12},{1,5},{5,9},{9,13},{2,6},{6,10},{10,14},{3,7},{... | collective-permute-start | bytes 786440 | tf_op jit(solution)/shard_map/while/body/eval_jaxpr/ppermute | solution.py:11
  157.8 9.6 %collective-permute-start = (f32[1,4,128,128]{3,2,1,0:T(8,128)S(1)}, f32[1,4,128,128]{3,2,1,0:T(8,128)S(1)}, u32[]{:S(2)}, u32[]{:S(2)}) collective-permute-start(f32[1,4,128,128]{3,2,1,0:T(8,128)S(1)} %multiply_add_fusion.3), channel_id=1, source_target_pairs={{0,4},{4,8},{8,12},{1,5},{5,9},{9,13},{2,6},{6,10},{10,14},{3,7},{... | collective-permute-start | bytes 786440 | tf_op jit(solution)/shard_map/while/body/eval_jaxpr/ppermute | solution.py:11
  167.5 8.7 %collective-permute-start = (f32[1,4,128,128]{3,2,1,0:T(8,128)S(1)}, f32[1,4,128,128]{3,2,1,0:T(8,128)S(1)}, u32[]{:S(2)}, u32[]{:S(2)}) collective-permute-start(f32[1,4,128,128]{3,2,1,0:T(8,128)S(1)} %multiply_add_fusion.3), channel_id=1, source_target_pairs={{0,4},{4,8},{8,12},{1,5},{5,9},{9,13},{2,6},{6,10},{10,14},{3,7},{... | collective-permute-start | bytes 786440 | tf_op jit(solution)/shard_map/while/body/eval_jaxpr/ppermute | solution.py:11
  180.3 62.0 %reduce-scatter.2.cloned.1.call-start = ((), (), s32[]{:S(2)}) async-start(), calls=%async_computation.7 | async-start | bytes 2621440 | tf_op jit(solution)/shard_map/reduce_scatter | solution.py:136
  197.1 74.0 %copy-start.3 = (bf16[1024,1024]{0,1:T(8,128)(2,1)S(1)}, bf16[1024,1024]{0,1:T(8,128)(2,1)}, u32[]{:S(2)}) copy-start(bf16[1024,1024]{0,1:T(8,128)(2,1)} %all-gather.9.cloned.1.call-done) | copy-start | bytes 6291460
  197.1 74.0 %all-gather.11.cloned.1.call-start = ((), (), s32[]{:S(2)}) async-start(), calls=%async_computation.6 | async-start | bytes 1310720 | tf_op jit(solution)/shard_map/all_gather | solution.py:84
  197.7 103.8 %all-reduce.2.cloned.1.call-start = ((), (), s32[]{:S(2)}) async-start(), calls=%async_computation.8 | async-start | bytes 1048576 | tf_op jit(solution)/shard_map/psum | solution.py:145
Sparse Core Ops, SparseCore 0:
  9.6 81.4 all-gather.4
  93.2 9.8 all-gather.6
  180.5 12.4 all-gather.8
  197.3 45.0 reduce-scatter.1
  243.8 27.2 all-gather.10
  273.4 28.0 all-reduce.1
where the time goes:
time: 311 us; the launch traced here: 310 us
  waiting for transfers between devices  151 us (49%)
  blocking collectives  56.2 us (18%)
  matrix products  31.1 us (10%)
  local copies, waits for them, and re-layouts  25.4 us (8%)
  starting transfers between devices  17.8 us (6%)
  between operations  15.5 us (5%)
  other arithmetic  10.4 us (3%)
    all_to_all x1, blocking collectives, local(): lax.all_to_all(latents, 'seq', split_axis=1, concat_axis=2, tiled=True)  56.2 us
    reduce_scatter x1, waiting for transfers between devices, local(): lax.psum_scatter(lax.dot_general(attn_full, cot_rows, (((0,), (0,)), ((),...  44.5 us
    all_gather x1, waiting for transfers between devices, local(): lax.all_gather(out_weight, 'seq', axis=0, tiled=True)  28.8 us
    psum x1, waiting for transfers between devices, local(): weight_grad = lax.psum(my_rows, 'dp')  26.9 us
    ppermute x3, waiting for transfers between devices, shifted(): lax.ppermute(value, axis, [(source, source + steps) for source in range(i...  15.4 us
    all_gather x1, waiting for transfers between devices, local(): lax.all_gather(qkv_weight, 'seq', axis=0, tiled=True)  13 us
    all_gather x1, waiting for transfers between devices, local(): attn_full = lax.all_gather(attn_rows, 'head', axis=1, tiled=True)  12.6 us
    ppermute x3, starting transfers between devices, shifted(): lax.ppermute(value, axis, [(source, source + steps) for source in range(i...  12.5 us
  transfers between devices with their start and end apart: 10, of which 10 were waited for; matrix products, arithmetic and copies ran while one was open for 5% of the time, Pallas kernels for 0%

commit v1 on v0

--- a/solution.py
+++ b/solution.py
@@ -74,13 +74,29 @@
 
 
 def local(latents, log_decay, seg_lengths, qkv_weight, out_weight, cotangent):
+
+    def derive_sizes_on(state, along_axis, out_dim=0):
+        n_lanes = lax.axis_size(along_axis)
+        log = tuple(((j0, (j0 + 1) % n_lanes) for j0 in range(n_lanes)))
+        shaped, local_now = ([state], [state])
+        buffer = tuple(((j0, (j0 - 1) % n_lanes) for j0 in range(n_lanes)))
+        for _ in range(n_lanes // 2):
+            shaped.append(lax.ppermute(shaped[-1], axis_name=along_axis, perm=log))
+        for _ in range((n_lanes - 1) // 2):
+            local_now.append(lax.ppermute(local_now[-1], axis_name=along_axis, perm=buffer))
+        opened = jnp.concatenate([*shaped[::-1], *local_now[1:]], out_dim)
+        block_now = jnp.roll(
+            opened, (lax.axis_index(along_axis) - n_lanes // 2) * state.shape[out_dim], out_dim
+        )
+        return block_now
+
     strips, rate_strips = (
         lax.all_to_all(latents, "seq", split_axis=1, concat_axis=2, tiled=True),
         lax.all_to_all(log_decay, "seq", split_axis=1, concat_axis=2, tiled=True),
     )
     features = lax.all_gather(strips, "head", axis=3, tiled=True)
     proj_full, out_full = (
-        lax.all_gather(qkv_weight, "seq", axis=0, tiled=True),
+        derive_sizes_on(qkv_weight, "seq"),
         lax.all_gather(out_weight, "seq", axis=0, tiled=True),
     )
     drives_here, rows_here, columns, feature_width = features.shape

time: 311 us -> 310 us (level)
  blocking collectives: 56.2 us -> 0 us
  waiting for transfers between devices: 151 us -> 186 us
  local copies, waits for them, and re-layouts: 25.4 us -> 34.8 us
  starting transfers between devices: 17.8 us -> 24.4 us
    all_to_all x1 -> x0, blocking collectives: 56.2 us -> none  [local(): lax.all_to_all(latents, 'seq', split_axis=1, concat_axis=2, tiled=True)]
    all_to_all x0 -> x1, waiting for transfers between devices: none -> 36.3 us  [local(): lax.all_to_all(latents, 'seq', split_axis=1, concat_axis=2, tiled=True)]
    ppermute x0 -> x3, waiting for transfers between devices: none -> 16.6 us  [the longest x2 16.6 us: derive_sizes_on(): shaped.append(lax.ppermute(shaped[-1], axis_name=along_axis, perm=log))]
    all_gather x1 -> x0, waiting for transfers between devices: 13 us -> none  [local(): lax.all_gather(qkv_weight, 'seq', axis=0, tiled=True)]
    all_to_all x1, waiting for transfers between devices: 1.38 us -> 9.55 us  [local(): lax.all_to_all(log_decay, 'seq', split_axis=1, concat_axis=2, tiled=True)]
    all_gather x1, waiting for transfers between devices: 7.31 us -> 0.01 us  [local(): features = lax.all_gather(strips, 'head', axis=3, tiled=True)]
    dynamic_slice x0 -> x2, local copies, waits for them, and re-layouts: none -> 6.59 us  [derive_sizes_on(): jnp.roll(opened, (lax.axis_index(along_axis) - n_lanes // 2) * state.shap...]
    all_to_all x0 -> x1, starting transfers between devices: none -> 6.46 us  [local(): lax.all_to_all(latents, 'seq', split_axis=1, concat_axis=2, tiled=True)]
  transfers between devices with their start and end apart: 10 -> 13, of which waited for: 10 -> 10; matrix products, arithmetic and copies ran while one was open for 5% -> 8% of each run, Pallas kernels for 0% -> 0%
where the time goes in v1:
time: 310 us; the launch traced here: 308 us
  waiting for transfers between devices  186 us (60%)
  local copies, waits for them, and re-layouts  34.8 us (11%)
  matrix products  33 us (11%)
  starting transfers between devices  24.4 us (8%)
  between operations  15.3 us (5%)
  other arithmetic  12.4 us (4%)
    reduce_scatter x1, waiting for transfers between devices, local(): lax.psum_scatter(lax.dot_general(attn_full, cot_rows, (((0,), (0,)), ((),...  44.6 us
    all_to_all x1, waiting for transfers between devices, local(): lax.all_to_all(latents, 'seq', split_axis=1, concat_axis=2, tiled=True)  36.3 us
    all_gather x1, waiting for transfers between devices, local(): lax.all_gather(out_weight, 'seq', axis=0, tiled=True)  28.7 us
    psum x1, waiting for transfers between devices, local(): weight_grad = lax.psum(my_rows, 'dp')  26.9 us
    ppermute x2, waiting for transfers between devices, derive_sizes_on(): shaped.append(lax.ppermute(shaped[-1], axis_name=along_axis, perm=log))  16.6 us
    ppermute x3, waiting for transfers between devices, shifted(): lax.ppermute(value, axis, [(source, source + steps) for source in range(i...  11.6 us
    all_gather x1, waiting for transfers between devices, local(): attn_full = lax.all_gather(attn_rows, 'head', axis=1, tiled=True)  11 us
    ppermute x3, starting transfers between devices, shifted(): lax.ppermute(value, axis, [(source, source + steps) for source in range(i...  10.1 us
  transfers between devices with their start and end apart: 13, of which 10 were waited for; matrix products, arithmetic and copies ran while one was open for 8% of the time, Pallas kernels for 0%

profile of v1, /device:TPU:0, one launch (start us, length us, event | category | flops | bytes accessed | tf_op | source)
XLA Modules:
  0.0 308.4 jit_solution(11740517687152217870)
XLA Ops:
  7.2 6.5 %all-to-all-start.1 = ((bf16[1,8,128,512]{3,2,0,1:T(8,128)(2,1)}), bf16[1,8,128,512]{3,2,0,1:T(8,128)(2,1)S(1)}, u32[]{:S(2)}, u32[]{:S(2)}) async-start(bf16[1,8,128,512]{3,2,0,1:T(8,128)(2,1)} %bitcast.208), calls=%async_computation.1 | async-start | bytes 2097152 | tf_op jit(solution)/shard_map/all_to_all | solution.py:94
  13.6 2.0 collective-permute-start.1
  15.7 1.8 collective-permute-start.3
  17.5 0.8 reduce_window_sum.81
  18.3 1.3 fusion.38
  19.7 0.6 slice.57
  21.0 36.3 %all-to-all-done.1 = bf16[1,8,128,512]{3,2,0,1:T(8,128)(2,1)S(1)} async-done(((bf16[1,8,128,512]{3,2,0,1:T(8,128)(2,1)}), bf16[1,8,128,512]{3,2,0,1:T(8,128)(2,1)S(1)}, u32[]{:S(2)}, u32[]{:S(2)}) %all-to-all-start.1) | async-done | bytes 1048608 | tf_op jit(solution)/shard_map/all_to_all | solution.py:94
  57.3 3.2 %all-to-all-start = ((bf16[1,8,128,4]{2,3,0,1:T(4,128)(2,1)}), bf16[1,8,128,4]{2,3,0,1:T(4,128)(2,1)S(1)}, u32[]{:S(2)}, u32[]{:S(2)}) async-start(bf16[1,8,128,4]{2,3,0,1:T(4,128)(2,1)} %bitcast.221), calls=%async_computation | async-start | bytes 16384 | tf_op jit(solution)/shard_map/all_to_all | solution.py:95
  60.6 0.7 add_bitcast_fusion
  61.3 0.6 slice.64
  62.6 1.1 copy.67
  63.7 9.5 %all-to-all-done = bf16[1,8,128,4]{2,3,0,1:T(4,128)(2,1)S(1)} async-done(((bf16[1,8,128,4]{2,3,0,1:T(4,128)(2,1)}), bf16[1,8,128,4]{2,3,0,1:T(4,128)(2,1)S(1)}, u32[]{:S(2)}, u32[]{:S(2)}) %all-to-all-start) | async-done | bytes 8224 | tf_op jit(solution)/shard_map/all_to_all | solution.py:95
  73.4 1.1 reduce-window.16
  74.5 1.0 copy.84
  76.5 0.8 broadcast.279
  77.4 1.2 copy.83
  78.6 0.7 multiply_bitcast_fusion
  79.3 16.6 %collective-permute-done.2 = bf16[256,3,512]{2,0,1:T(8,128)(2,1)} collective-permute-done((bf16[256,3,512]{2,0,1:T(8,128)(2,1)}, bf16[256,3,512]{2,0,1:T(8,128)(2,1)}, u32[]{:S(2)}, u32[]{:S(2)}) %collective-permute-start.2) | collective-permute-done | bytes 786464 | tf_op jit(solution)/shard_map/ppermute | solution.py:84
  95.9 1.2 constant_dynamic-update-slice_fusion.7
  97.1 1.2 constant_dynamic-update-slice_fusion.6
  98.4 1.2 constant_dynamic-update-slice_fusion.3
  99.6 1.2 constant_dynamic-update-slice_fusion.2
  100.9 1.9 constant_dynamic-slice_fusion.6
  102.8 4.7 %copy.65 = bf16[1024,3,512]{0,2,1:T(8,128)(2,1)} copy(bf16[1024,3,512]{2,0,1:T(8,128)(2,1)} %constant_dynamic-slice_fusion.6) | data formatting | bytes 6291456 | tf_op jit(solution)/shard_map/jit(_roll_dynamic)/dynamic_slice | solution.py:88
  107.5 6.0 %convert_bitcast_fusion = bf16[3,1,4,2,512,128]{4,5,3,2,0,1:T(8,128)(2,1)S(1)} fusion(bf16[1024,3,4,128,1]{0,3,4,2,1:T(8,128)(2,1)} %bitcast.204, bf16[1,2,512,1024]{3,2,1,0:T(8,128)(2,1)} %all-gather.4.cloned.1.call-done), kind=kOutput, calls=%fused_computation.48 | convolution fusion | flops 3222798336 | bytes 8388608 | tf_op jit(solution)/shard_map/bsaf,fchd->cbhsad/dot_general | solution.py:108
  113.5 2.2 fusion.41
  115.7 31.0 %while.24 = (s32[]{:T(128)}, f32[1,4,128,128]{3,2,1,0:T(8,128)S(1)}, f32[2,1,4,512,128]{4,3,2,1,0:T(8,128)}, f32[2,1,4,512]{3,2,1,0:T(4,128)S(1)}, s32[2,1,512]{...) while((s32[]{:T(128)}, ...), condition=%wide.region_6.7_spmd.clone, body=%wide.region_3.6_spmd.clone.sunk | while | flops 1015816256 | bytes 9897850 | solution.py:60
  115.7 0.6 constant_dynamic-slice_fusion.13
  116.3 0.6 compare_convert_fusion.6
  117.0 1.2 reduce-window.26
  119.1 3.5 %fusion.69 = f32[4,512,128]{2,1,0:T(8,128)S(1)} fusion(f32[4,512]{1,0:T(4,128)S(1)} %get-tuple-element.263, pred[512,512]{1,0:T(8,128)(4,1)S(1)} %fusion.68, bf16[2,1,4,512,128]{3,4,0,2,1:T(8,128)(2,1)} %get-tuple-element.299, s32[]{:T(128)} %get-tuple-element.279, bf16[2,1,4,512,128]{3,4,0,2,1:T(8,128)(2,1)} %get-tuple-element.298, ...), kind=kOutput, calls=%fused_computation.2.clone.1 | convolution fusion | flops 543162368 | bytes 2901504 | tf_op jit(solution)/shard_map/vmap()/while/body/eval_jaxpr/hts,hsd->htd/dot_general | solution.py:24
  122.6 2.8 fusion.70
  125.4 0.6 slice.92
  127.4 0.6 compare_convert_fusion.7
  128.0 1.1 constant_dynamic-slice_fusion.11
  129.4 1.9 fusion.67
  131.3 0.6 constant_dynamic-slice_fusion.13
  131.9 0.6 compare_convert_fusion.6
  132.6 1.2 reduce-window.26
  134.6 3.5 %fusion.69 = f32[4,512,128]{2,1,0:T(8,128)S(1)} fusion(f32[4,512]{1,0:T(4,128)S(1)} %get-tuple-element.263, pred[512,512]{1,0:T(8,128)(4,1)S(1)} %fusion.68, bf16[2,1,4,512,128]{3,4,0,2,1:T(8,128)(2,1)} %get-tuple-element.299, s32[]{:T(128)} %get-tuple-element.279, bf16[2,1,4,512,128]{3,4,0,2,1:T(8,128)(2,1)} %get-tuple-element.298, ...), kind=kOutput, calls=%fused_computation.2.clone.1 | convolution fusion | flops 543162368 | bytes 2901504 | tf_op jit(solution)/shard_map/vmap()/while/body/eval_jaxpr/hts,hsd->htd/dot_general | solution.py:24
  138.1 2.8 fusion.70
  140.9 0.6 slice.92
  142.9 0.6 compare_convert_fusion.7
  143.5 1.1 constant_dynamic-slice_fusion.11
  144.9 1.9 fusion.67
  146.8 2.9 copy.72
  149.7 2.9 reshape.615
  152.5 1.6 copy.76
  154.2 22.0 %while.23 = (s32[]{:T(128)}, f32[1,4,128,128]{3,2,1,0:T(8,128)S(1)}, f32[1,4]{1,0:T(1,128)S(1)}, f32[1,4,128,128]{3,2,1,0:T(8,128)S(1)}, s32[]{:T(128)}) while((s32[]{:T(128)}, f32[1,4,128,128]{3,2,1,0:T(8,128)S(1)}, f32[1,4]{1,0:T(1,128)S(1)}, f32[1,4,128,128]{3,2,1,0:T(8,128)S(1)}, s32[]{:T(128)}) %tuple.57), condition=%wide.region_10.11_spmd, body=%wide.region_9.10_spmd.sunk | while | flops 131074 | bytes 1835125 | solution.py:131
  154.3 1.3 collective-permute-start
  155.6 3.9 %collective-permute-done = f32[1,4,128,128]{3,2,1,0:T(8,128)S(1)} collective-permute-done((f32[1,4,128,128]{3,2,1,0:T(8,128)S(1)}, f32[1,4,128,128]{3,2,1,0:T(8,128)S(1)}, u32[]{:S(2)}, u32[]{:S(2)}) %collective-permute-start) | collective-permute-done | bytes 262176 | tf_op jit(solution)/shard_map/while/body/eval_jaxpr/ppermute | solution.py:11
  159.5 4.4 %collective-permute-start = (f32[1,4,128,128]{3,2,1,0:T(8,128)S(1)}, f32[1,4,128,128]{3,2,1,0:T(8,128)S(1)}, u32[]{:S(2)}, u32[]{:S(2)}) collective-permute-start(f32[1,4,128,128]{3,2,1,0:T(8,128)S(1)} %multiply_add_fusion.3), channel_id=1, source_target_pairs={{0,4},{4,8},{8,12},{1,5},{5,9},{9,13},{2,6},{6,10},{10,14},{3,7},{... | collective-permute-start | bytes 786440 | tf_op jit(solution)/shard_map/while/body/eval_jaxpr/ppermute | solution.py:11
  164.0 3.9 %collective-permute-done = f32[1,4,128,128]{3,2,1,0:T(8,128)S(1)} collective-permute-done((f32[1,4,128,128]{3,2,1,0:T(8,128)S(1)}, f32[1,4,128,128]{3,2,1,0:T(8,128)S(1)}, u32[]{:S(2)}, u32[]{:S(2)}) %collective-permute-start) | collective-permute-done | bytes 262176 | tf_op jit(solution)/shard_map/while/body/eval_jaxpr/ppermute | solution.py:11
  167.9 4.4 %collective-permute-start = (f32[1,4,128,128]{3,2,1,0:T(8,128)S(1)}, f32[1,4,128,128]{3,2,1,0:T(8,128)S(1)}, u32[]{:S(2)}, u32[]{:S(2)}) collective-permute-start(f32[1,4,128,128]{3,2,1,0:T(8,128)S(1)} %multiply_add_fusion.3), channel_id=1, source_target_pairs={{0,4},{4,8},{8,12},{1,5},{5,9},{9,13},{2,6},{6,10},{10,14},{3,7},{... | collective-permute-start | bytes 786440 | tf_op jit(solution)/shard_map/while/body/eval_jaxpr/ppermute | solution.py:11
  172.3 3.9 %collective-permute-done = f32[1,4,128,128]{3,2,1,0:T(8,128)S(1)} collective-permute-done((f32[1,4,128,128]{3,2,1,0:T(8,128)S(1)}, f32[1,4,128,128]{3,2,1,0:T(8,128)S(1)}, u32[]{:S(2)}, u32[]{:S(2)}) %collective-permute-start) | collective-permute-done | bytes 262176 | tf_op jit(solution)/shard_map/while/body/eval_jaxpr/ppermute | solution.py:11
  176.2 2.9 multiply_reduce_fusion
  179.1 1.2 multiply_convert_fusion.3
  180.4 11.0 %all-gather.6.cloned.1.call-done = bf16[1024,1024]{0,1:T(8,128)(2,1)} async-done(((bf16[1024,512]{0,1:T(8,128)(2,1)}), bf16[1024,1024]{0,1:T(8,128)(2,1)}) %all-gather.6.cloned.1.call-update) | async-done | bytes 2097168 | tf_op jit(solution)/shard_map/all_gather | solution.py:145
  191.3 4.3 %convolution_multiply_fusion.1 = f32[1024,512]{1,0:T(8,128)} fusion(bf16[1024,1024]{0,1:T(8,128)(2,1)} %all-gather.6.cloned.1.call-done, bf16[1024,512]{1,0:T(8,128)(2,1)S(1)} %bitcast.196), kind=kOutput, calls=%fused_computation.53 | convolution fusion | flops 1074266112 | bytes 5242880 | tf_op jit(solution)/shard_map/dot_general | solution.py:153
  196.3 44.6 %reduce-scatter.2.cloned.1.call-done = f32[256,512]{1,0:T(8,128)} async-done(((f32[1024,512]{1,0:T(8,128)}), f32[256,512]{1,0:T(8,128)}) %reduce-scatter.2.cloned.1.call-update) | async-done | bytes 524304 | tf_op jit(solution)/shard_map/reduce_scatter | solution.py:152
  240.9 28.7 %all-gather.8.cloned.1.call-done = bf16[1024,512]{1,0:T(8,128)(2,1)} async-done(((bf16[256,512]{1,0:T(8,128)(2,1)}), bf16[1024,512]{1,0:T(8,128)(2,1)}) %all-gather.8.cloned.1.call-update) | async-done | bytes 1048592 | tf_op jit(solution)/shard_map/all_gather | solution.py:100
  269.6 3.5 %convolution_convert_fusion = bf16[1024,512]{1,0:T(8,128)(2,1)} fusion(bf16[1024,1024]{0,1:T(8,128)(2,1)S(1)} %copy-done.2, bf16[1024,512]{1,0:T(8,128)(2,1)} %all-gather.8.cloned.1.call-done), kind=kOutput, calls=%fused_computation.54 | convolution fusion | flops 1074266112 | bytes 4194304 | tf_op jit(solution)/shard_map/dot_general | solution.py:146
  273.1 26.9 %all-reduce.2.cloned.1.call-done = f32[256,512]{1,0:T(8,128)} async-done(((f32[256,512]{1,0:T(8,128)}), f32[256,512]{1,0:T(8,128)}) %all-reduce.2.cloned.1.call-update) | async-done | bytes 524304 | tf_op jit(solution)/shard_map/psum | solution.py:161
  300.0 1.9 copy.130
  (78 shorter events, 5.2 us)
Async XLA Ops:
  7.2 184.2 %copy-start = (bf16[1,2,512,512]{3,2,1,0:T(8,128)(2,1)S(1)}, bf16[1,2,512,512]{3,2,1,0:T(8,128)(2,1)}, u32[]{:S(2)}) copy-start(bf16[1,2,512,512]{3,2,1,0:T(8,128)(2,1)} %param.15) | copy-start | bytes 3145732
  7.2 50.1 %all-to-all-start.1 = ((bf16[1,8,128,512]{3,2,0,1:T(8,128)(2,1)}), bf16[1,8,128,512]{3,2,0,1:T(8,128)(2,1)S(1)}, u32[]{:S(2)}, u32[]{:S(2)}) async-start(bf16[1,8,128,512]{3,2,0,1:T(8,128)(2,1)} %bitcast.208), calls=%async_computation.1 | async-start | bytes 2097152 | tf_op jit(solution)/shard_map/all_to_all | solution.py:94
  13.6 61.9 %collective-permute-start.1 = (bf16[256,3,512]{2,0,1:T(8,128)(2,1)}, bf16[256,3,512]{2,0,1:T(8,128)(2,1)}, u32[]{:S(2)}, u32[]{:S(2)}) collective-permute-start(bf16[256,3,512]{2,0,1:T(8,128)(2,1)} %param.13), channel_id=1, source_target_pairs={{0,4},{4,8},{8,12},{12,0},{1,5},{5,9},{9,13},{13,1},{2,6},{6,10},{... | collective-permute-start | bytes 2359304 | tf_op jit(solution)/shard_map/ppermute | solution.py:84
  15.7 82.7 %collective-permute-start.3 = (bf16[256,3,512]{2,0,1:T(8,128)(2,1)}, bf16[256,3,512]{2,0,1:T(8,128)(2,1)S(1)}, u32[]{:S(2)}, u32[]{:S(2)}) collective-permute-start(bf16[256,3,512]{2,0,1:T(8,128)(2,1)} %param.13), channel_id=1, source_target_pairs={{0,12},{4,0},{8,4},{12,8},{1,13},{5,1},{9,5},{13,9},{2,14},{6,2},{... | collective-permute-start | bytes 2359304 | tf_op jit(solution)/shard_map/ppermute | solution.py:86
  57.3 16.0 %all-to-all-start = ((bf16[1,8,128,4]{2,3,0,1:T(4,128)(2,1)}), bf16[1,8,128,4]{2,3,0,1:T(4,128)(2,1)S(1)}, u32[]{:S(2)}, u32[]{:S(2)}) async-start(bf16[1,8,128,4]{2,3,0,1:T(4,128)(2,1)} %bitcast.221), calls=%async_computation | async-start | bytes 16384 | tf_op jit(solution)/shard_map/all_to_all | solution.py:95
  60.6 46.9 %all-gather.4.cloned.1.call-start = ((), (), s32[]{:S(2)}) async-start(), calls=%async_computation.3 | async-start | bytes 3145728 | tf_op jit(solution)/shard_map/all_gather | solution.py:97
  63.7 34.6 %copy-start.1 = (bf16[256,3,512]{2,0,1:T(8,128)(2,1)S(1)}, bf16[256,3,512]{2,0,1:T(8,128)(2,1)}, u32[]{:S(2)}) copy-start(bf16[256,3,512]{2,0,1:T(8,128)(2,1)} %param.13) | copy-start | bytes 2359300
  63.7 127.7 %all-gather.6.cloned.1.call-start = ((), (), s32[]{:S(2)}) async-start(), calls=%async_computation.4 | async-start | bytes 3145728 | tf_op jit(solution)/shard_map/all_gather | solution.py:145
  75.6 20.3 %collective-permute-start.2 = (bf16[256,3,512]{2,0,1:T(8,128)(2,1)}, bf16[256,3,512]{2,0,1:T(8,128)(2,1)}, u32[]{:S(2)}, u32[]{:S(2)}) collective-permute-start(bf16[256,3,512]{2,0,1:T(8,128)(2,1)} %collective-permute-done.1), channel_id=1, source_target_pairs={{0,4},{4,8},{8,12},{12,0},{1,5},{5,9},{9,13},{13,1},{2,6},{6,10},{... | collective-permute-start | bytes 2359304 | tf_op jit(solution)/shard_map/ppermute | solution.py:84
  154.3 5.2 %collective-permute-start = (f32[1,4,128,128]{3,2,1,0:T(8,128)S(1)}, f32[1,4,128,128]{3,2,1,0:T(8,128)S(1)}, u32[]{:S(2)}, u32[]{:S(2)}) collective-permute-start(f32[1,4,128,128]{3,2,1,0:T(8,128)S(1)} %multiply_add_fusion.3), channel_id=1, source_target_pairs={{0,4},{4,8},{8,12},{1,5},{5,9},{9,13},{2,6},{6,10},{10,14},{3,7},{... | collective-permute-start | bytes 786440 | tf_op jit(solution)/shard_map/while/body/eval_jaxpr/ppermute | solution.py:11
  159.5 8.3 %collective-permute-start = (f32[1,4,128,128]{3,2,1,0:T(8,128)S(1)}, f32[1,4,128,128]{3,2,1,0:T(8,128)S(1)}, u32[]{:S(2)}, u32[]{:S(2)}) collective-permute-start(f32[1,4,128,128]{3,2,1,0:T(8,128)S(1)} %multiply_add_fusion.3), channel_id=1, source_target_pairs={{0,4},{4,8},{8,12},{1,5},{5,9},{9,13},{2,6},{6,10},{10,14},{3,7},{... | collective-permute-start | bytes 786440 | tf_op jit(solution)/shard_map/while/body/eval_jaxpr/ppermute | solution.py:11
  167.9 8.3 %collective-permute-start = (f32[1,4,128,128]{3,2,1,0:T(8,128)S(1)}, f32[1,4,128,128]{3,2,1,0:T(8,128)S(1)}, u32[]{:S(2)}, u32[]{:S(2)}) collective-permute-start(f32[1,4,128,128]{3,2,1,0:T(8,128)S(1)} %multiply_add_fusion.3), channel_id=1, source_target_pairs={{0,4},{4,8},{8,12},{1,5},{5,9},{9,13},{2,6},{6,10},{10,14},{3,7},{... | collective-permute-start | bytes 786440 | tf_op jit(solution)/shard_map/while/body/eval_jaxpr/ppermute | solution.py:11
  180.3 60.5 %reduce-scatter.2.cloned.1.call-start = ((), (), s32[]{:S(2)}) async-start(), calls=%async_computation.6 | async-start | bytes 2621440 | tf_op jit(solution)/shard_map/reduce_scatter | solution.py:152
  191.3 78.3 %copy-start.2 = (bf16[1024,1024]{0,1:T(8,128)(2,1)S(1)}, bf16[1024,1024]{0,1:T(8,128)(2,1)}, u32[]{:S(2)}) copy-start(bf16[1024,1024]{0,1:T(8,128)(2,1)} %all-gather.6.cloned.1.call-done) | copy-start | bytes 6291460
  195.7 74.0 %all-gather.8.cloned.1.call-start = ((), (), s32[]{:S(2)}) async-start(), calls=%async_computation.5 | async-start | bytes 1310720 | tf_op jit(solution)/shard_map/all_gather | solution.py:100
  196.2 103.8 %all-reduce.2.cloned.1.call-start = ((), (), s32[]{:S(2)}) async-start(), calls=%async_computation.7 | async-start | bytes 1048576 | tf_op jit(solution)/shard_map/psum | solution.py:161
Sparse Core Ops, SparseCore 0:
  63.8 11.9 all-gather.3
  180.4 10.8 all-gather.5
  195.8 45.0 reduce-scatter.1
  242.4 27.2 all-gather.7
  271.9 28.0 all-reduce.1
